TPU v7x, 256 devices: a whole 4x4x8 slice. The times are simulated.
256 devices in a mesh: dp: 16 (over z_hi, y, core), expert: 16 (over x, z_lo).
Axes of the slice: x: 4, y: 4, z: 8 (z_hi: 2, z_lo: 4; z = z_hi * 4 + z_lo), core: 2. Of those that a mesh axis runs over, the one named last changes fastest.
Arguments:
- layer_inputs: bfloat16 [32768, 2560], P(('dp', 'expert')), may hold values from -6 to 6
- cotangent: bfloat16 [32768, 2560], P(('dp', 'expert')), may hold values from -3 to 3
- expert_ids: int32 [32768, 3], P(('dp', 'expert')), may hold values from 0 to 15, all different within a row; in each aligned block of 128 rows (0 to 127, 128 to 255, ...) at most 26 rows name the same one
- route_weights: bfloat16 [32768, 3], P(('dp', 'expert')), may hold values from 0.049804688 to 0.59765625
- w_gate_up: bfloat16 [16, 2560, 1536], P('expert'), may hold values from -0.125 to 0.125
- w_down: bfloat16 [16, 768, 2560], P('expert', None, 'dp'), may hold values from -0.21875 to 0.21875
Outputs:
- input_grad: bfloat16 [32768, 2560], P(('dp', 'expert'))
- gate_grad: bfloat16 [32768, 3], P(('dp', 'expert'))
- grad_gate_up: bfloat16 [16, 2560, 1536], P('expert', 'dp')
- grad_down: bfloat16 [16, 768, 2560], P('expert', None, 'dp')
Inputs may be any that keep to these rules, and one draw needn't show every extreme that they name: `expert_ids`: each row names 3 different experts; among the rows of one device no expert is named by more than 26 rows.
All inputs are finite; a program needn't handle non-finite values.
Results may differ from a plain program's by a relative error of at most 0.019.
Values may be sent and summed in bfloat16 or wider, within the bound.
No kernel may reach another device: no remote copies, remote signals or barrier semaphores. Data moves between devices by JAX's collectives and lax.ppermute only.
A program may use at most 128 MiB of HBM per device.

v0:
```python
import jax
import jax.numpy as jnp
from jax import lax
from jax.sharding import PartitionSpec as P


def on_device(layer_inputs, cotangent, expert_ids, route_weights, w_gate_up, w_down):
    tok_rows, feat_width = layer_inputs.shape
    top_count = expert_ids.shape[1]
    expert_count = lax.axis_size("expert")
    capacity = tok_rows * top_count // expert_count * 13 // 12
    pair_count = tok_rows * top_count
    slot_total = expert_count * capacity
    hidden_width = w_down.shape[1]
    chosen_ids = expert_ids.reshape(-1)
    one_hot = (chosen_ids[:, None] == jnp.arange(expert_count, dtype=jnp.int32)[None, :]).astype(
        jnp.int32
    )
    pair_rank = jnp.sum((jnp.cumsum(one_hot, axis=0) - one_hot) * one_hot, axis=1)
    pair_slot = chosen_ids * capacity + pair_rank
    slot_owner = (
        jnp.full((slot_total,), -1, jnp.int32)
        .at[pair_slot]
        .set(jnp.arange(pair_count, dtype=jnp.int32))
    )
    filled = slot_owner >= 0
    owner_safe = jnp.where(filled, slot_owner, 0)
    source_token = owner_safe // top_count
    zero_bf = jnp.zeros((), jnp.bfloat16)
    rows_out = jnp.where(filled[:, None], layer_inputs[source_token], zero_bf).reshape(
        expert_count, capacity, feat_width
    )
    cot_out = jnp.where(filled[:, None], cotangent[source_token], zero_bf).reshape(
        expert_count, capacity, feat_width
    )
    gate_out = jnp.where(filled, route_weights.reshape(-1)[owner_safe], zero_bf).reshape(
        expert_count, capacity
    )
    rows_in, cot_in, gate_in = (
        lax.all_to_all(rows_out, "expert", split_axis=0, concat_axis=0, tiled=True),
        lax.all_to_all(cot_out, "expert", split_axis=0, concat_axis=0, tiled=True),
        lax.all_to_all(gate_out, "expert", split_axis=0, concat_axis=0, tiled=True),
    )
    expert_rows = rows_in.reshape(slot_total, feat_width)
    gate_up = w_gate_up[0]
    projected = jnp.dot(expert_rows, gate_up, preferred_element_type=jnp.float32)
    gate_pre = projected[:, :hidden_width]
    up_pre = projected[:, hidden_width:]
    sigmoid_gate = jax.nn.sigmoid(gate_pre)
    silu_gate = gate_pre * sigmoid_gate
    hidden = (silu_gate * up_pre).astype(jnp.bfloat16)
    expert_cot = cot_in.reshape(slot_total, feat_width)
    expert_gate = gate_in.reshape(slot_total)
    out_grad = (expert_gate.astype(jnp.float32)[:, None] * expert_cot.astype(jnp.float32)).astype(
        jnp.bfloat16
    )
    col_block = lax.all_gather(w_down, "dp", axis=2, tiled=True)[0]
    out_part = jnp.dot(hidden, col_block, preferred_element_type=jnp.float32)
    gate_dot = jnp.sum(expert_cot.astype(jnp.float32) * out_part, axis=1)
    hidden_grad = lax.dot_general(
        out_grad, col_block, (((1,), (1,)), ((), ())), preferred_element_type=jnp.float32
    )
    gate_dot, hidden_grad = (gate_dot, hidden_grad)
    pre_grad = jnp.concatenate(
        [
            hidden_grad * up_pre * sigmoid_gate * (1.0 + gate_pre * (1.0 - sigmoid_gate)),
            hidden_grad * silu_gate,
        ],
        axis=1,
    ).astype(jnp.bfloat16)
    row_grads = lax.dot_general(
        pre_grad, gate_up, (((1,), (1,)), ((), ())), preferred_element_type=jnp.float32
    ).astype(jnp.bfloat16)
    back_rows, back_dots = (
        lax.all_to_all(
            row_grads.reshape(expert_count, capacity, feat_width),
            "expert",
            split_axis=0,
            concat_axis=0,
            tiled=True,
        ),
        lax.all_to_all(
            gate_dot.astype(jnp.bfloat16).reshape(expert_count, capacity),
            "expert",
            split_axis=0,
            concat_axis=0,
            tiled=True,
        ),
    )
    pair_grads = (
        back_rows.reshape(slot_total, feat_width)[pair_slot]
        .astype(jnp.float32)
        .reshape(tok_rows, top_count, feat_width)
    )
    input_grad = jnp.sum(pair_grads, axis=1).astype(jnp.bfloat16)
    gate_grad = back_dots.reshape(-1)[pair_slot].reshape(tok_rows, top_count)
    gu_grad = lax.psum_scatter(
        lax.dot_general(
            expert_rows, pre_grad, (((0,), (0,)), ((), ())), preferred_element_type=jnp.float32
        ).astype(jnp.bfloat16),
        "dp",
        scatter_dimension=0,
        tiled=True,
    )
    down_local = lax.dot_general(
        hidden, out_grad, (((0,), (0,)), ((), ())), preferred_element_type=jnp.float32
    )
    down_grad = lax.psum_scatter(
        down_local.astype(jnp.bfloat16), "dp", scatter_dimension=1, tiled=True
    )
    return (input_grad, gate_grad, gu_grad[None], down_grad[None])


def solution(mesh):
    placed = (
        P(("dp", "expert"), None),
        P(("dp", "expert"), None),
        P(("dp", "expert"), None),
        P(("dp", "expert"), None),
        P("expert", None, None),
        P("expert", None, "dp"),
    )
    return jax.shard_map(
        on_device,
        mesh=mesh,
        in_specs=placed,
        out_specs=(
            P(("dp", "expert"), None),
            P(("dp", "expert"), None),
            P("expert", "dp", None),
            P("expert", None, "dp"),
        ),
        check_vma=False,
    )
```

profile of v0, /device:TPU:34, one launch (start us, length us, event | category | flops | bytes accessed | tf_op | source)
XLA Modules:
  0.0 492.9 jit_solution(5862637363636940772)
XLA Ops:
  7.2 0.0 copy-start
  7.2 0.8 broadcast_multiply_fusion
  7.9 0.8 copy.24
  8.7 0.2 eq.29
  8.9 0.2 eq.25
  9.1 0.8 copy.27
  9.9 0.2 reshape.130
  10.2 0.1 copy.23
  10.3 0.2 mul.58
  10.5 0.9 reduce-window.6
  11.4 0.2 slice_reduce_fusion
  11.6 0.1 fusion.17
  11.8 2.9 scatter_custom_fusion
  14.7 3.2 gather_fusion
  17.9 0.7 all_to_all.25
  18.6 8.5 %all-to-all-start = ((bf16[16,1,26]{2,1,0:T(2,128)(2,1)}), bf16[16,1,26]{2,1,0:T(2,128)(2,1)S(1)}, u32[]{:S(2)}, u32[]{:S(2)}) async-start(bf16[16,1,26]{2,1,0:T(2,128)(2,1)} %all_to_all.25), calls=%async_computation | async-start | bytes 16384 | tf_op jit(solution)/shard_map/all_to_all | solution.py:42
  27.1 0.1 broadcast_in_dim.50
  27.2 0.0 copy-done
  27.2 3.4 gather_fusion.2
  30.6 2.7 gather.25
  33.3 0.0 copy-done.2
  33.3 3.4 gather_fusion.1
  36.7 4.1 gather.23
  40.8 4.5 broadcast_select_fusion
  45.3 0.0 all-to-all-done
  45.3 7.5 %all-to-all-start.1 = ((bf16[16,26,2560]{2,1,0:T(8,128)(2,1)}), bf16[16,26,2560]{2,1,0:T(8,128)(2,1)S(1)}, u32[]{:S(2)}, u32[]{:S(2)}) async-start(bf16[16,26,2560]{2,1,0:T(8,128)(2,1)} %get-tuple-element.22), calls=%async_computation.1 | async-start | bytes 5242880 | tf_op jit(solution)/shard_map/all_to_all | solution.py:41
  52.8 0.0 all-gather.2.cloned.1.call-start
  52.8 0.7 all-gather.2.cloned.1.call-update
  53.5 60.2 %all-to-all-done.1 = bf16[16,26,2560]{2,1,0:T(8,128)(2,1)S(1)} async-done(((bf16[16,26,2560]{2,1,0:T(8,128)(2,1)}), bf16[16,26,2560]{2,1,0:T(8,128)(2,1)S(1)}, u32[]{:S(2)}, u32[]{:S(2)}) %all-to-all-start.1) | async-done | bytes 2129952 | tf_op jit(solution)/shard_map/all_to_all | solution.py:41
  113.7 9.6 %all-to-all-start.2 = ((bf16[16,26,2560]{2,1,0:T(8,128)(2,1)}), bf16[16,26,2560]{2,1,0:T(8,128)(2,1)}, u32[]{:S(2)}, u32[]{:S(2)}) async-start(bf16[16,26,2560]{2,1,0:T(8,128)(2,1)} %get-tuple-element.21), calls=%async_computation.2 | async-start | bytes 5242880 | tf_op jit(solution)/shard_map/all_to_all | solution.py:40
  123.3 0.2 reduce-scatter.5.cloned.1.call-start
  123.6 0.1 reshape.138
  123.7 2.0 multiply_convert_fusion
  125.7 4.1 convert_element_type.77
  129.8 2.7 reshape.137
  132.5 60.1 %all-to-all-done.2 = bf16[16,26,2560]{2,1,0:T(8,128)(2,1)} async-done(((bf16[16,26,2560]{2,1,0:T(8,128)(2,1)}), bf16[16,26,2560]{2,1,0:T(8,128)(2,1)}, u32[]{:S(2)}, u32[]{:S(2)}) %all-to-all-start.2) | async-done | bytes 2129952 | tf_op jit(solution)/shard_map/all_to_all | solution.py:40
  192.6 2.8 reshape.131
  195.3 7.3 %fusion.2 = f32[416,1536]{1,0:T(8,128)} fusion(bf16[416,2560]{1,0:T(8,128)(2,1)S(1)} %reshape.131, bf16[1,2560,1536]{2,1,0:T(8,128)(2,1)} %param.10), kind=kOutput, calls=%fused_computation.9 | convolution fusion | flops 3271557120 | bytes 12550144 | tf_op jit(solution)/shard_map/dot_general | solution.py:46
  202.6 6.8 %multiply_convert_fusion.5 = (bf16[416,768]{1,0:T(8,128)(2,1)}, bf16[416,768]{1,0:T(8,128)(2,1)}, bf16[416,768]{1,0:T(8,128)(2,1)S(1)}) fusion(f32[416,1536]{1,0:T(8,128)} %fusion.2, bf16[416,2560]{1,0:T(8,128)(2,1)} %convert_element_type.77, bf16[1,768,2560]{1,2,0:T(8,128)(2,1)} %all-gather.2.cloned.1.call-done), kind=kOutput, calls=%fused_computation.26 | convolution fusion | flops 1640570880 | bytes 10534912 | tf_op jit(solution)/shard_map/dot_general | solution.py:60
  209.4 0.0 copy-done.3
  209.4 4.3 convolution_convert_fusion.1
  213.6 0.0 reduce-scatter.5.cloned.1.call-update
  213.7 0.0 reduce-scatter.3.cloned.1.call-start
  213.7 7.7 %convolution_convert_fusion = bf16[2560,1536]{1,0:T(8,128)(2,1)} fusion(bf16[416,2560]{1,0:T(8,128)(2,1)S(1)} %reshape.131, bf16[416,768]{1,0:T(8,128)(2,1)} %get-tuple-element.19, bf16[416,768]{1,0:T(8,128)(2,1)} %get-tuple-element.18), kind=kOutput, calls=%fused_computation.6 | convolution fusion | flops 3278045184 | bytes 11272192 | tf_op jit(solution)/shard_map/dot_general | solution.py:98
  221.4 0.0 reduce-scatter.3.cloned.1.call-update
  221.5 5.4 %fusion.11 = bf16[416]{0:T(512)(128)(2,1)S(1)} fusion(f32[416,2560]{1,0:T(8,128)} %reshape.137, bf16[416,768]{1,0:T(8,128)(2,1)S(1)} %get-tuple-element.20, bf16[1,768,2560]{1,2,0:T(8,128)(2,1)} %all-gather.2.cloned.1.call-done), kind=kOutput, calls=%fused_computation.22 | convolution fusion | flops 1637908096 | bytes 8831808 | tf_op jit(solution)/shard_map/dot_general | solution.py:58
  226.9 0.7 convert_element_type.92
  227.6 10.3 %all-to-all-start.4 = ((bf16[16,1,26]{2,1,0:T(2,128)(2,1)}), bf16[16,1,26]{2,1,0:T(2,128)(2,1)S(1)}, u32[]{:S(2)}, u32[]{:S(2)}) async-start(bf16[16,1,26]{2,1,0:T(2,128)(2,1)} %convert_element_type.92), calls=%async_computation.4 | async-start | bytes 16384 | tf_op jit(solution)/shard_map/all_to_all | solution.py:82
  237.8 7.6 %fusion.4 = bf16[416,2560]{1,0:T(8,128)(2,1)S(1)} fusion(bf16[1,2560,1536]{2,1,0:T(8,128)(2,1)} %param.10, bf16[416,768]{1,0:T(8,128)(2,1)} %get-tuple-element.19, bf16[416,768]{1,0:T(8,128)(2,1)} %get-tuple-element.18), kind=kOutput, calls=%fused_computation.14 | convolution fusion | flops 3275177984 | bytes 11272192 | tf_op jit(solution)/shard_map/dot_general | solution.py:71
  245.4 2.3 reshape.132
  247.8 0.0 all-to-all-done.4
  247.8 7.6 %all-to-all-start.3 = ((bf16[16,26,2560]{2,1,0:T(8,128)(2,1)}), bf16[16,26,2560]{2,1,0:T(8,128)(2,1)}, u32[]{:S(2)}, u32[]{:S(2)}) async-start(bf16[16,26,2560]{2,1,0:T(8,128)(2,1)} %reshape.132), calls=%async_computation.3 | async-start | bytes 5242880 | tf_op jit(solution)/shard_map/all_to_all | solution.py:75
  255.4 0.1 reshape.134
  255.5 2.8 gather_fusion.4
  258.3 0.2 reshape.135
  258.5 0.7 copy.30
  259.2 75.9 %all-to-all-done.3 = bf16[16,26,2560]{2,1,0:T(8,128)(2,1)} async-done(((bf16[16,26,2560]{2,1,0:T(8,128)(2,1)}), bf16[16,26,2560]{2,1,0:T(8,128)(2,1)}, u32[]{:S(2)}, u32[]{:S(2)}) %all-to-all-start.3) | async-done | bytes 2129952 | tf_op jit(solution)/shard_map/all_to_all | solution.py:75
  335.1 2.8 reshape.133
  337.9 3.3 gather_fusion.3
  341.2 4.4 gather.27
  345.6 4.3 reduce_sum.34
  349.9 1.8 reduce-scatter.5.cloned.1.call-done
  351.8 134.6 %reduce-scatter.3.cloned.1.call-done = bf16[160,1536]{1,0:T(8,128)(2,1)} async-done(((bf16[2560,1536]{1,0:T(8,128)(2,1)}), bf16[160,1536]{1,0:T(8,128)(2,1)}) %reduce-scatter.3.cloned.1.call-update) | async-done | bytes 491536 | tf_op jit(solution)/shard_map/reduce_scatter | solution.py:97
  486.4 0.0 copy-done.1
  (17 shorter events, 0.2 us)
Async XLA Ops:
  7.2 20.0 %copy-start = (bf16[128,2560]{1,0:T(8,128)(2,1)S(1)}, bf16[128,2560]{1,0:T(8,128)(2,1)}, u32[]{:S(2)}) copy-start(bf16[128,2560]{1,0:T(8,128)(2,1)} %param.6) | copy-start | bytes 1966084
  18.6 26.6 %all-to-all-start = ((bf16[16,1,26]{2,1,0:T(2,128)(2,1)}), bf16[16,1,26]{2,1,0:T(2,128)(2,1)S(1)}, u32[]{:S(2)}, u32[]{:S(2)}) async-start(bf16[16,1,26]{2,1,0:T(2,128)(2,1)} %all_to_all.25), calls=%async_computation | async-start | bytes 16384 | tf_op jit(solution)/shard_map/all_to_all | solution.py:42
  30.6 2.7 copy-start.2
  45.3 68.4 %all-to-all-start.1 = ((bf16[16,26,2560]{2,1,0:T(8,128)(2,1)}), bf16[16,26,2560]{2,1,0:T(8,128)(2,1)S(1)}, u32[]{:S(2)}, u32[]{:S(2)}) async-start(bf16[16,26,2560]{2,1,0:T(8,128)(2,1)} %get-tuple-element.22), calls=%async_computation.1 | async-start | bytes 5242880 | tf_op jit(solution)/shard_map/all_to_all | solution.py:41
  52.8 149.8 %all-gather.2.cloned.1.call-start = ((), (), s32[]{:S(2)}) async-start(), calls=%async_computation.7 | async-start | bytes 4177920 | tf_op jit(solution)/shard_map/all_gather | solution.py:57
  113.7 78.9 %all-to-all-start.2 = ((bf16[16,26,2560]{2,1,0:T(8,128)(2,1)}), bf16[16,26,2560]{2,1,0:T(8,128)(2,1)}, u32[]{:S(2)}, u32[]{:S(2)}) async-start(bf16[16,26,2560]{2,1,0:T(8,128)(2,1)} %get-tuple-element.21), calls=%async_computation.2 | async-start | bytes 5242880 | tf_op jit(solution)/shard_map/all_to_all | solution.py:40
  123.3 228.5 %reduce-scatter.5.cloned.1.call-start = ((), (), s32[]{:S(2)}) async-start(), calls=%async_computation.9 | async-start | bytes 4177920 | tf_op jit(solution)/shard_map/reduce_scatter | solution.py:108
  202.6 6.8 %copy-start.3 = (f32[416,2560]{1,0:T(8,128)S(1)}, f32[416,2560]{1,0:T(8,128)}, u32[]{:S(2)}) copy-start(f32[416,2560]{1,0:T(8,128)} %reshape.137) | copy-start | bytes 12779524
  213.7 272.7 %reduce-scatter.3.cloned.1.call-start = ((), (), s32[]{:S(2)}) async-start(), calls=%async_computation.8 | async-start | bytes 8355840 | tf_op jit(solution)/shard_map/reduce_scatter | solution.py:97
  227.6 20.2 %all-to-all-start.4 = ((bf16[16,1,26]{2,1,0:T(2,128)(2,1)}), bf16[16,1,26]{2,1,0:T(2,128)(2,1)S(1)}, u32[]{:S(2)}, u32[]{:S(2)}) async-start(bf16[16,1,26]{2,1,0:T(2,128)(2,1)} %convert_element_type.92), calls=%async_computation.4 | async-start | bytes 16384 | tf_op jit(solution)/shard_map/all_to_all | solution.py:82
  247.8 87.4 %all-to-all-start.3 = ((bf16[16,26,2560]{2,1,0:T(8,128)(2,1)}), bf16[16,26,2560]{2,1,0:T(8,128)(2,1)}, u32[]{:S(2)}, u32[]{:S(2)}) async-start(bf16[16,26,2560]{2,1,0:T(8,128)(2,1)} %reshape.132), calls=%async_computation.3 | async-start | bytes 5242880 | tf_op jit(solution)/shard_map/all_to_all | solution.py:75
  341.2 145.2 %copy-start.1 = (bf16[128,2560]{1,0:T(8,128)(2,1)S(1)}, bf16[128,2560]{1,0:T(8,128)(2,1)}, u32[]{:S(2)}) copy-start(bf16[128,2560]{1,0:T(8,128)(2,1)} %param.6) | copy-start | bytes 1966084
Sparse Core Ops, SparseCore 0:
  56.3 101.2 all-gather.1
  213.8 137.9 reduce-scatter.4
  356.9 129.4 reduce-scatter.2
where the time goes:
time: 495 us; the launch traced here: 493 us
  waiting for transfers between devices  333 us (67%)
  local copies, waits for them, and re-layouts  50.1 us (10%)
  starting transfers between devices  43.7 us (9%)
  matrix products  39 us (8%)
  between operations  13.9 us (3%)
  other arithmetic  12.7 us (3%)
    reduce_scatter x1, waiting for transfers between devices, on_device(): lax.psum_scatter(lax.dot_general(expert_rows, pre_grad, (((0,), (0,)), ((...  135 us
    all_to_all x1, waiting for transfers between devices, on_device(): lax.all_to_all(row_grads.reshape(expert_count, capacity, feat_width), 'ex...  75.9 us
    all_to_all x1, waiting for transfers between devices, on_device(): lax.all_to_all(cot_out, 'expert', split_axis=0, concat_axis=0, tiled=True)  60.2 us
    all_to_all x1, waiting for transfers between devices, on_device(): lax.all_to_all(rows_out, 'expert', split_axis=0, concat_axis=0, tiled=True)  60.1 us
    all_to_all x1, starting transfers between devices, on_device(): lax.all_to_all(gate_dot.astype(jnp.bfloat16).reshape(expert_count, capaci...  10.3 us
  transfers between devices with their start and end apart: 8, of which 5 were waited for; matrix products, arithmetic and copies ran while one was open for 16% of the time, Pallas kernels for 0%

commit v1 on v0

--- a/solution.py
+++ b/solution.py
@@ -13,10 +13,9 @@
     slot_total = expert_count * capacity
     hidden_width = w_down.shape[1]
     chosen_ids = expert_ids.reshape(-1)
-    one_hot = (chosen_ids[:, None] == jnp.arange(expert_count, dtype=jnp.int32)[None, :]).astype(
-        jnp.int32
-    )
-    pair_rank = jnp.sum((jnp.cumsum(one_hot, axis=0) - one_hot) * one_hot, axis=1)
+    order = jnp.arange(pair_count, dtype=jnp.int32)
+    earlier = (chosen_ids[:, None] == chosen_ids[None, :]) & (order[None, :] < order[:, None])
+    pair_rank = jnp.sum(earlier.astype(jnp.int32), axis=1)
     pair_slot = chosen_ids * capacity + pair_rank
     slot_owner = (
         jnp.full((slot_total,), -1, jnp.int32)

time: 495 us -> 494 us (level)
  no operation moved by 1% of the time
where the time goes in v1:
time: 494 us; the launch traced here: 492 us
  waiting for transfers between devices  333 us (67%)
  local copies, waits for them, and re-layouts  49.7 us (10%)
  starting transfers between devices  43.6 us (9%)
  matrix products  39 us (8%)
  between operations  13.9 us (3%)
  other arithmetic  11.9 us (2%)
    reduce_scatter x1, waiting for transfers between devices, on_device(): lax.psum_scatter(lax.dot_general(expert_rows, pre_grad, (((0,), (0,)), ((...  135 us
    all_to_all x1, waiting for transfers between devices, on_device(): lax.all_to_all(row_grads.reshape(expert_count, capacity, feat_width), 'ex...  76 us
    all_to_all x1, waiting for transfers between devices, on_device(): lax.all_to_all(cot_out, 'expert', split_axis=0, concat_axis=0, tiled=True)  60.2 us
    all_to_all x1, waiting for transfers between devices, on_device(): lax.all_to_all(rows_out, 'expert', split_axis=0, concat_axis=0, tiled=True)  60.1 us
    all_to_all x1, starting transfers between devices, on_device(): lax.all_to_all(gate_dot.astype(jnp.bfloat16).reshape(expert_count, capaci...  10.2 us
  transfers between devices with their start and end apart: 8, of which 5 were waited for; matrix products, arithmetic and copies ran while one was open for 16% of the time, Pallas kernels for 0%

profile of v1, /device:TPU:34, one launch (start us, length us, event | category | flops | bytes accessed | tf_op | source)
XLA Modules:
  0.0 491.6 jit_solution(6623882579553748787)
XLA Ops:
  7.2 0.0 copy-start
  7.2 0.8 broadcast_multiply_fusion
  7.9 0.8 copy.26
  8.7 0.8 copy.27
  9.5 0.2 reshape.114
  9.7 0.1 copy.25
  9.9 0.2 mul.55
  10.1 0.2 eq.15
  10.3 0.2 convert_reduce_fusion
  10.6 2.9 scatter_custom_fusion
  13.5 3.2 gather_fusion
  16.7 0.7 all_to_all.25
  17.4 8.5 %all-to-all-start = ((bf16[16,1,26]{2,1,0:T(2,128)(2,1)}), bf16[16,1,26]{2,1,0:T(2,128)(2,1)S(1)}, u32[]{:S(2)}, u32[]{:S(2)}) async-start(bf16[16,1,26]{2,1,0:T(2,128)(2,1)} %all_to_all.25), calls=%async_computation | async-start | bytes 16384 | tf_op jit(solution)/shard_map/all_to_all | solution.py:41
  25.9 0.1 broadcast_in_dim.51
  26.0 0.0 copy-done
  26.0 3.4 gather_fusion.2
  29.4 0.0 copy-start.2
  29.4 2.7 gather.25
  32.1 0.0 copy-done.2
  32.1 3.4 gather_fusion.1
  35.4 4.1 gather.23
  39.6 4.5 broadcast_select_fusion
  44.0 0.0 all-to-all-done
  44.0 7.5 %all-to-all-start.1 = ((bf16[16,26,2560]{2,1,0:T(8,128)(2,1)}), bf16[16,26,2560]{2,1,0:T(8,128)(2,1)S(1)}, u32[]{:S(2)}, u32[]{:S(2)}) async-start(bf16[16,26,2560]{2,1,0:T(8,128)(2,1)} %get-tuple-element.26), calls=%async_computation.1 | async-start | bytes 5242880 | tf_op jit(solution)/shard_map/all_to_all | solution.py:40
  51.6 0.0 all-gather.2.cloned.1.call-start
  51.6 0.7 all-gather.2.cloned.1.call-update
  52.3 60.2 %all-to-all-done.1 = bf16[16,26,2560]{2,1,0:T(8,128)(2,1)S(1)} async-done(((bf16[16,26,2560]{2,1,0:T(8,128)(2,1)}), bf16[16,26,2560]{2,1,0:T(8,128)(2,1)S(1)}, u32[]{:S(2)}, u32[]{:S(2)}) %all-to-all-start.1) | async-done | bytes 2129952 | tf_op jit(solution)/shard_map/all_to_all | solution.py:40
  112.5 9.6 %all-to-all-start.2 = ((bf16[16,26,2560]{2,1,0:T(8,128)(2,1)}), bf16[16,26,2560]{2,1,0:T(8,128)(2,1)}, u32[]{:S(2)}, u32[]{:S(2)}) async-start(bf16[16,26,2560]{2,1,0:T(8,128)(2,1)} %get-tuple-element.25), calls=%async_computation.2 | async-start | bytes 5242880 | tf_op jit(solution)/shard_map/all_to_all | solution.py:39
  122.1 0.2 reduce-scatter.5.cloned.1.call-start
  122.3 0.1 reshape.122
  122.4 2.0 multiply_convert_fusion
  124.4 4.1 convert_element_type.72
  128.6 2.7 reshape.121
  131.2 60.1 %all-to-all-done.2 = bf16[16,26,2560]{2,1,0:T(8,128)(2,1)} async-done(((bf16[16,26,2560]{2,1,0:T(8,128)(2,1)}), bf16[16,26,2560]{2,1,0:T(8,128)(2,1)}, u32[]{:S(2)}, u32[]{:S(2)}) %all-to-all-start.2) | async-done | bytes 2129952 | tf_op jit(solution)/shard_map/all_to_all | solution.py:39
  191.3 2.8 reshape.115
  194.1 7.3 %fusion.2 = f32[416,1536]{1,0:T(8,128)} fusion(bf16[416,2560]{1,0:T(8,128)(2,1)S(1)} %reshape.115, bf16[1,2560,1536]{2,1,0:T(8,128)(2,1)} %param.10), kind=kOutput, calls=%fused_computation.9 | convolution fusion | flops 3271557120 | bytes 12550144 | tf_op jit(solution)/shard_map/dot_general | solution.py:45
  201.4 0.0 all-gather.2.cloned.1.call-done
  201.4 0.0 copy-start.3
  201.4 6.8 %multiply_convert_fusion.5 = (bf16[416,768]{1,0:T(8,128)(2,1)}, bf16[416,768]{1,0:T(8,128)(2,1)}, bf16[416,768]{1,0:T(8,128)(2,1)S(1)}) fusion(f32[416,1536]{1,0:T(8,128)} %fusion.2, bf16[416,2560]{1,0:T(8,128)(2,1)} %convert_element_type.72, bf16[1,768,2560]{1,2,0:T(8,128)(2,1)} %all-gather.2.cloned.1.call-done), kind=kOutput, calls=%fused_computation.26 | convolution fusion | flops 1640570880 | bytes 10534912 | tf_op jit(solution)/shard_map/dot_general | solution.py:59
  208.2 0.0 copy-done.3
  208.2 4.3 convolution_convert_fusion.1
  212.4 0.0 reduce-scatter.5.cloned.1.call-update
  212.4 0.0 reduce-scatter.3.cloned.1.call-start
  212.5 7.7 %convolution_convert_fusion = bf16[2560,1536]{1,0:T(8,128)(2,1)} fusion(bf16[416,2560]{1,0:T(8,128)(2,1)S(1)} %reshape.115, bf16[416,768]{1,0:T(8,128)(2,1)} %get-tuple-element.23, bf16[416,768]{1,0:T(8,128)(2,1)} %get-tuple-element.22), kind=kOutput, calls=%fused_computation.6 | convolution fusion | flops 3278045184 | bytes 11272192 | tf_op jit(solution)/shard_map/dot_general | solution.py:97
  220.2 0.0 reduce-scatter.3.cloned.1.call-update
  220.2 5.4 %fusion.11 = bf16[416]{0:T(512)(128)(2,1)S(1)} fusion(f32[416,2560]{1,0:T(8,128)} %reshape.121, bf16[416,768]{1,0:T(8,128)(2,1)S(1)} %get-tuple-element.24, bf16[1,768,2560]{1,2,0:T(8,128)(2,1)} %all-gather.2.cloned.1.call-done), kind=kOutput, calls=%fused_computation.22 | convolution fusion | flops 1637908096 | bytes 8831808 | tf_op jit(solution)/shard_map/dot_general | solution.py:57
  225.6 0.7 convert_element_type.87
  226.3 10.2 %all-to-all-start.4 = ((bf16[16,1,26]{2,1,0:T(2,128)(2,1)}), bf16[16,1,26]{2,1,0:T(2,128)(2,1)S(1)}, u32[]{:S(2)}, u32[]{:S(2)}) async-start(bf16[16,1,26]{2,1,0:T(2,128)(2,1)} %convert_element_type.87), calls=%async_computation.4 | async-start | bytes 16384 | tf_op jit(solution)/shard_map/all_to_all | solution.py:81
  236.5 7.6 %fusion.4 = bf16[416,2560]{1,0:T(8,128)(2,1)S(1)} fusion(bf16[1,2560,1536]{2,1,0:T(8,128)(2,1)} %param.10, bf16[416,768]{1,0:T(8,128)(2,1)} %get-tuple-element.23, bf16[416,768]{1,0:T(8,128)(2,1)} %get-tuple-element.22), kind=kOutput, calls=%fused_computation.14 | convolution fusion | flops 3275177984 | bytes 11272192 | tf_op jit(solution)/shard_map/dot_general | solution.py:70
  244.1 2.3 reshape.116
  246.4 0.0 all-to-all-done.4
  246.4 7.5 %all-to-all-start.3 = ((bf16[16,26,2560]{2,1,0:T(8,128)(2,1)}), bf16[16,26,2560]{2,1,0:T(8,128)(2,1)}, u32[]{:S(2)}, u32[]{:S(2)}) async-start(bf16[16,26,2560]{2,1,0:T(8,128)(2,1)} %reshape.116), calls=%async_computation.3 | async-start | bytes 5242880 | tf_op jit(solution)/shard_map/all_to_all | solution.py:74
  254.0 0.1 reshape.118
  254.1 2.8 gather_fusion.4
  256.9 0.2 reshape.119
  257.2 0.7 copy.30
  257.8 76.0 %all-to-all-done.3 = bf16[16,26,2560]{2,1,0:T(8,128)(2,1)} async-done(((bf16[16,26,2560]{2,1,0:T(8,128)(2,1)}), bf16[16,26,2560]{2,1,0:T(8,128)(2,1)}, u32[]{:S(2)}, u32[]{:S(2)}) %all-to-all-start.3) | async-done | bytes 2129952 | tf_op jit(solution)/shard_map/all_to_all | solution.py:74
  333.8 2.8 reshape.117
  336.6 3.3 gather_fusion.3
  339.9 4.4 gather.27
  344.3 4.3 reduce_sum.34
  348.6 1.9 reduce-scatter.5.cloned.1.call-done
  350.5 134.6 %reduce-scatter.3.cloned.1.call-done = bf16[160,1536]{1,0:T(8,128)(2,1)} async-done(((bf16[2560,1536]{1,0:T(8,128)(2,1)}), bf16[160,1536]{1,0:T(8,128)(2,1)}) %reduce-scatter.3.cloned.1.call-update) | async-done | bytes 491536 | tf_op jit(solution)/shard_map/reduce_scatter | solution.py:96
  485.1 0.0 copy-done.1
  (12 shorter events, 0.2 us)
Async XLA Ops:
  7.2 18.8 %copy-start = (bf16[128,2560]{1,0:T(8,128)(2,1)S(1)}, bf16[128,2560]{1,0:T(8,128)(2,1)}, u32[]{:S(2)}) copy-start(bf16[128,2560]{1,0:T(8,128)(2,1)} %param.6) | copy-start | bytes 1966084
  17.4 26.6 %all-to-all-start = ((bf16[16,1,26]{2,1,0:T(2,128)(2,1)}), bf16[16,1,26]{2,1,0:T(2,128)(2,1)S(1)}, u32[]{:S(2)}, u32[]{:S(2)}) async-start(bf16[16,1,26]{2,1,0:T(2,128)(2,1)} %all_to_all.25), calls=%async_computation | async-start | bytes 16384 | tf_op jit(solution)/shard_map/all_to_all | solution.py:41
  29.4 2.7 copy-start.2
  44.0 68.4 %all-to-all-start.1 = ((bf16[16,26,2560]{2,1,0:T(8,128)(2,1)}), bf16[16,26,2560]{2,1,0:T(8,128)(2,1)S(1)}, u32[]{:S(2)}, u32[]{:S(2)}) async-start(bf16[16,26,2560]{2,1,0:T(8,128)(2,1)} %get-tuple-element.26), calls=%async_computation.1 | async-start | bytes 5242880 | tf_op jit(solution)/shard_map/all_to_all | solution.py:40
  51.6 149.8 %all-gather.2.cloned.1.call-start = ((), (), s32[]{:S(2)}) async-start(), calls=%async_computation.7 | async-start | bytes 4177920 | tf_op jit(solution)/shard_map/all_gather | solution.py:56
  112.5 78.9 %all-to-all-start.2 = ((bf16[16,26,2560]{2,1,0:T(8,128)(2,1)}), bf16[16,26,2560]{2,1,0:T(8,128)(2,1)}, u32[]{:S(2)}, u32[]{:S(2)}) async-start(bf16[16,26,2560]{2,1,0:T(8,128)(2,1)} %get-tuple-element.25), calls=%async_computation.2 | async-start | bytes 5242880 | tf_op jit(solution)/shard_map/all_to_all | solution.py:39
  122.1 228.4 %reduce-scatter.5.cloned.1.call-start = ((), (), s32[]{:S(2)}) async-start(), calls=%async_computation.9 | async-start | bytes 4177920 | tf_op jit(solution)/shard_map/reduce_scatter | solution.py:107
  201.4 6.8 %copy-start.3 = (f32[416,2560]{1,0:T(8,128)S(1)}, f32[416,2560]{1,0:T(8,128)}, u32[]{:S(2)}) copy-start(f32[416,2560]{1,0:T(8,128)} %reshape.121) | copy-start | bytes 12779524
  212.4 272.6 %reduce-scatter.3.cloned.1.call-start = ((), (), s32[]{:S(2)}) async-start(), calls=%async_computation.8 | async-start | bytes 8355840 | tf_op jit(solution)/shard_map/reduce_scatter | solution.py:96
  226.3 20.1 %all-to-all-start.4 = ((bf16[16,1,26]{2,1,0:T(2,128)(2,1)}), bf16[16,1,26]{2,1,0:T(2,128)(2,1)S(1)}, u32[]{:S(2)}, u32[]{:S(2)}) async-start(bf16[16,1,26]{2,1,0:T(2,128)(2,1)} %convert_element_type.87), calls=%async_computation.4 | async-start | bytes 16384 | tf_op jit(solution)/shard_map/all_to_all | solution.py:81
  246.4 87.4 %all-to-all-start.3 = ((bf16[16,26,2560]{2,1,0:T(8,128)(2,1)}), bf16[16,26,2560]{2,1,0:T(8,128)(2,1)}, u32[]{:S(2)}, u32[]{:S(2)}) async-start(bf16[16,26,2560]{2,1,0:T(8,128)(2,1)} %reshape.116), calls=%async_computation.3 | async-start | bytes 5242880 | tf_op jit(solution)/shard_map/all_to_all | solution.py:74
  339.9 145.2 %copy-start.1 = (bf16[128,2560]{1,0:T(8,128)(2,1)S(1)}, bf16[128,2560]{1,0:T(8,128)(2,1)}, u32[]{:S(2)}) copy-start(bf16[128,2560]{1,0:T(8,128)(2,1)} %param.6) | copy-start | bytes 1966084
Sparse Core Ops, SparseCore 0:
  55.1 101.1 all-gather.1
  212.6 137.8 reduce-scatter.4
  355.6 129.4 reduce-scatter.2
